TPU v7x, 512 devices: a whole 4x4x16 slice. The times are simulated.
512 devices in a mesh: date: 32 (over y_lo, z), row: 16 (over x, y_hi, core).
Axes of the slice: x: 4, y: 4 (y_hi: 2, y_lo: 2; y = y_hi * 2 + y_lo), z: 16, core: 2. Of those that a mesh axis runs over, the one named last changes fastest.
Arguments:
- slc: bfloat16 [2, 128, 256, 1024], P(None, 'date', 'row'), may hold values from -64 to 64
Outputs:
- coherence: float32 [2, 128, 128, 32, 128], P(None, 'date', None, 'row')
All inputs are finite; a program needn't handle non-finite values.
Results may differ from a plain program's by a relative error of at most 0.0013.
Values may be sent and summed in bfloat16 or wider, within the bound.
No kernel may reach another device: no remote copies, remote signals or barrier semaphores. Data moves between devices by JAX's collectives and lax.ppermute only.
A program may use at most 64 MiB of HBM per device.

v0:
```python
import jax
import jax.numpy as jnp
from jax import lax
from jax.sharding import PartitionSpec as P


def padded(array, sides, width):
    for axis, dim in sides:
        size, length = (lax.axis_size(axis), array.shape[dim])
        up = [(i, (i + 1) % size) for i in range(size - 1)]
        down = [(j, i) for i, j in up]
        last = lax.slice_in_dim(array, length - width, length, axis=dim)
        initial = lax.slice_in_dim(array, 0, width, axis=dim)
        before = lax.ppermute(last, axis, up)
        after = lax.ppermute(initial, axis, down)
        array = jnp.concatenate([before, array, after], axis=dim)
    return array


def window_matrix(inputs, outputs, offset):
    target = lax.broadcasted_iota(jnp.int32, (outputs, inputs), 0)
    source = lax.broadcasted_iota(jnp.int32, (outputs, inputs), 1)
    lowest = 8 * target + offset
    return ((source >= lowest) & (source <= lowest + 14)).astype(jnp.float32)


def pair_sums(own_block, other_block, rows_filter, cols_filter):
    own_re = own_block[0].astype(jnp.float32)[:, None]
    own_im = own_block[1].astype(jnp.float32)[:, None]
    other_re = other_block[0].astype(jnp.float32)[None]
    other_im = other_block[1].astype(jnp.float32)[None]
    real_part = (own_re * other_re + own_im * other_im).astype(jnp.bfloat16)
    imag_part = (own_im * other_re - own_re * other_im).astype(jnp.bfloat16)
    products = jnp.stack([real_part, imag_part])
    across = jnp.einsum(
        "kijrc,cx->kijrx", products, cols_filter, preferred_element_type=jnp.float32
    )
    return jnp.einsum("yr,kijrx->kijyx", rows_filter, across, precision=lax.Precision.HIGHEST)


def pair_blocks(own_block, other_block, rows_filter, cols_filter):
    number = other_block.shape[1]

    def one_group(group):
        single = lax.dynamic_slice_in_dim(other_block, group * 16, 16, 1)
        return pair_sums(own_block, single, rows_filter, cols_filter)

    pieces = lax.map(one_group, jnp.arange(number // 16))
    pieces = jnp.moveaxis(pieces, 0, 2)
    return pieces.reshape(2, own_block.shape[1], number, pieces.shape[-2], pieces.shape[-1])


def on_device(slc):
    own_dates = slc.shape[1]
    strip_rows = slc.shape[2]
    columns = slc.shape[3]
    out_rows = strip_rows // 8
    out_cols = columns // 8
    stacked = padded(slc, (("row", 2),), 4)
    row_offset = 1
    rows_filter = window_matrix(stacked.shape[2], out_rows, row_offset)
    position = lax.axis_index("date")
    cols_filter = window_matrix(columns, out_cols, -3).T.astype(jnp.bfloat16)
    partial_value = pair_blocks(
        stacked, lax.all_gather(stacked, "date", axis=1, tiled=True), rows_filter, cols_filter
    )
    first_date = position * own_dates
    mine = lax.dynamic_slice_in_dim(partial_value[0], first_date, own_dates, 1)
    own_power = jnp.moveaxis(jnp.diagonal(mine, axis1=0, axis2=1), -1, 0)
    all_power = lax.all_gather(own_power, "date", axis=0, tiled=True)
    own_scale = lax.rsqrt(own_power + 1e-06)
    all_scale = lax.rsqrt(all_power + 1e-06)
    return partial_value * own_scale[None, :, None] * all_scale[None, None, :]


def solution(mesh):
    return jax.shard_map(
        on_device,
        mesh=mesh,
        in_specs=(P(None, "date", "row", None),),
        out_specs=P(None, "date", None, "row", None),
        check_vma=False,
    )
```

profile of v0, /device:TPU:2, one launch (start us, length us, event | category | flops | bytes accessed | tf_op | source)
XLA Modules:
  0.0 319.3 jit_solution(3863041069771411113)
XLA Ops:
  7.6 1.9 collective-permute-start
  9.5 6.0 %collective-permute-start.1 = (bf16[2,4,4,1024]{3,2,1,0:T(4,128)(2,1)S(1)}, bf16[2,4,4,1024]{3,2,1,0:T(4,128)(2,1)S(1)}, u32[]{:S(2)}, u32[]{:S(2)}) collective-permute-start(bf16[2,4,4,1024]{3,2,1,0:T(4,128)(2,1)S(1)} %get-tuple-element.93), channel_id=1, source_target_pairs={{1,0},{2,1},{3,2},{4,3},{5,4},{6,5},{7,6},{8,7},{9,8},{10,9},{11,1... | collective-permute-start | bytes 196616 | tf_op jit(solution)/shard_map/ppermute | solution.py:15
  15.6 1.9 collective-permute-done.1
  17.4 1.9 pad_maximum_fusion
  19.4 165.4 %all-gather.2.cloned.1.call-done = bf16[2,128,24,1024]{3,2,1,0:T(8,128)(2,1)} async-done(((bf16[2,4,24,1024]{3,2,1,0:T(8,128)(2,1)}), bf16[2,128,24,1024]{3,2,1,0:T(8,128)(2,1)}) %all-gather.2.cloned.1.call-update) | async-done | bytes 12582928 | tf_op jit(solution)/shard_map/all_gather | solution.py:65
  184.7 63.2 %while.11 = (s32[]{:T(128)}, f32[8,2,4,16,2,128]{5,3,0,4,2,1:T(8,128)S(1)}, bf16[2,4,24,1024]{3,2,1,0:T(8,128)(2,1)}, s32[8]{0:T(128)S(1)}, bf16[2,128,24,1024]{...) while((s32[]{:T(128)}, ...), condition=%wide.region_1.2_spmd.clone, body=%wide.region_0.1_spmd.clone.sunk | while | flops 832110784 | bytes 27526404 | solution.py:48
  187.9 1.9 add_convert_fusion.2
  189.7 1.9 fusion.39
  195.8 1.9 add_convert_fusion.2
  197.7 1.9 fusion.39
  203.7 1.9 add_convert_fusion.2
  205.6 1.9 fusion.39
  211.6 1.9 add_convert_fusion.2
  213.5 1.9 fusion.39
  219.5 1.9 add_convert_fusion.2
  221.4 1.9 fusion.39
  227.4 1.9 add_convert_fusion.2
  229.3 1.9 fusion.39
  235.3 1.9 add_convert_fusion.2
  237.2 1.9 fusion.39
  243.2 1.9 add_convert_fusion.2
  245.1 1.9 fusion.39
  248.7 61.8 %all_gather.7 = f32[128,2,128]{2,1,0:T(2,128)S(1)} all-gather(f32[4,2,128]{2,1,0:T(2,128)S(1)} %gather_fusion), channel_id=1, replica_groups=mesh['date'=32,'row'=16] {'date'}, dimensions={0}, use_global_device_ids=true | all-gather | bytes 135168 | tf_op jit(solution)/shard_map/all_gather | solution.py:70
  310.6 1.8 fusion.21
  (71 shorter events, 28.8 us)
Async XLA Ops:
  6.5 178.2 %all-gather.2.cloned.1.call-start = ((), (), s32[]{:S(2)}) async-start(), calls=%async_computation | async-start | bytes 12976128 | tf_op jit(solution)/shard_map/all_gather | solution.py:65
  7.6 8.0 %collective-permute-start = (bf16[2,4,4,1024]{3,2,1,0:T(4,128)(2,1)S(1)}, bf16[2,4,4,1024]{3,2,1,0:T(4,128)(2,1)S(1)}, u32[]{:S(2)}, u32[]{:S(2)}) collective-permute-start(bf16[2,4,4,1024]{3,2,1,0:T(4,128)(2,1)S(1)} %get-tuple-element.92), channel_id=1, source_target_pairs={{0,1},{1,2},{2,3},{3,4},{4,5},{5,6},{6,7},{7,8},{8,9},{9,10},{10,1... | collective-permute-start | bytes 196616 | tf_op jit(solution)/shard_map/ppermute | solution.py:14
  9.5 7.9 %collective-permute-start.1 = (bf16[2,4,4,1024]{3,2,1,0:T(4,128)(2,1)S(1)}, bf16[2,4,4,1024]{3,2,1,0:T(4,128)(2,1)S(1)}, u32[]{:S(2)}, u32[]{:S(2)}) collective-permute-start(bf16[2,4,4,1024]{3,2,1,0:T(4,128)(2,1)S(1)} %get-tuple-element.93), channel_id=1, source_target_pairs={{1,0},{2,1},{3,2},{4,3},{5,4},{6,5},{7,6},{8,7},{9,8},{10,9},{11,1... | collective-permute-start | bytes 196616 | tf_op jit(solution)/shard_map/ppermute | solution.py:15
  184.7 3.0 copy-start
  192.6 3.0 copy-start
  200.5 3.0 copy-start
  208.5 3.0 copy-start
  216.4 3.0 copy-start
  224.3 3.0 copy-start
  232.2 3.0 copy-start
  240.1 3.0 copy-start
Sparse Core Ops, SparseCore 0:
  19.4 165.2 all-gather.1
where the time goes:
time: 320 us; the launch traced here: 319 us
  waiting for transfers between devices  167 us (52%)
  blocking collectives  61.8 us (19%)
  other arithmetic  33.5 us (10%)
  matrix products  22.7 us (7%)
  between operations  13.5 us (4%)
  starting transfers between devices  7.97 us (2%)
  local copies, waits for them, and re-layouts  6.77 us (2%)
  loops' own time  5.76 us (2%)
    all_gather x1, waiting for transfers between devices, on_device(): lax.all_gather(stacked, 'date', axis=1, tiled=True)  165 us
    all_gather x1, blocking collectives, on_device(): all_power = lax.all_gather(own_power, 'date', axis=0, tiled=True)  61.8 us
    dot_general x8, matrix products, pair_sums(): jnp.einsum('kijrc,cx->kijrx', products, cols_filter, preferred_element_ty...  15.3 us
    convert_element_type x8, other arithmetic, pair_sums(): real_part = (own_re * other_re + own_im * other_im).astype(jnp.bfloat16)  15.1 us
    mul x8, other arithmetic, pair_sums(): real_part = (own_re * other_re + own_im * other_im).astype(jnp.bfloat16)  14 us
    dot_general x8, matrix products, pair_sums(): jnp.einsum('yr,kijrx->kijyx', rows_filter, across, precision=lax.Precisio...  7.35 us
  transfers between devices with their start and end apart: 3, of which 2 were waited for; matrix products, arithmetic and copies ran while one was open for 0% of the time, Pallas kernels for 0%

commit v1 on v0

v1 whole, which is shorter than its diff:
```python
import jax
import jax.numpy as jnp
import numpy as np
from jax import lax
from jax.experimental import pallas as pl
from jax.experimental.pallas import tpu as pltpu
from jax.sharding import PartitionSpec as P

BF16 = jnp.bfloat16
F32 = jnp.float32
LANES = 128
TILES = 5


def iota(shape, axis):
    return lax.broadcasted_iota(jnp.int32, shape, axis)


def butterfly(vregs, group, lane):
    count = len(vregs)
    step = 1
    while step < count:
        upper = (lane // group) & step != 0
        shift = group * step
        for i in range(count):
            if i & step:
                continue
            a, b = vregs[i], vregs[i + step]
            vregs[i] = jnp.where(upper, pltpu.roll(b, shift, 1), a)
            vregs[i + step] = jnp.where(upper, b, pltpu.roll(a, LANES - shift, 1))
        step *= 2
    return vregs


def pack_kernel(own_ref, out_ref):
    dates = own_ref.shape[0] // 16
    chunks = own_ref.shape[1] // LANES
    parts = out_ref.shape[0] // dates
    even = lax.axis_index("row") % 2 == 0
    lane = iota((dates, LANES), 1)
    target, source = iota((16 * dates, 16 * dates), 0), iota((16 * dates, 16 * dates), 1)
    order = (source == target % dates * 16 + target // dates).astype(F32).astype(BF16)
    bands = [[] for _ in range(4)]
    for c in range(0, chunks, 2):
        block = own_ref[:, LANES * c:LANES * (c + 2)]
        moved = jnp.dot(order, block, preferred_element_type=F32)
        for half in range(2):
            chunk = moved[:, LANES * half:LANES * (half + 1)]
            for g in range(4):
                rows = [chunk[dates * r:dates * (r + 1)] for r in range(4 * g, 4 * g + 4)]
                bands[g] += butterfly(rows, 32, lane)
    zero = jnp.zeros((dates, LANES), F32)
    low = lane % 8 < 4
    slot = jnp.where(low, lane // 8 % 4, (lane // 8 + 1) % 4)
    for j in range(parts):
        edge = None
        for g in range(4):
            after = zero if j == parts - 1 else bands[g][j + 1]
            before = zero if j == 0 else bands[g][j - 1]
            both = jnp.where(low, after, before)
            both = pltpu.roll(both, 8 * g, 1) if g else both
            edge = both if edge is None else jnp.where(slot == g, both, edge)
        first, last = bands[0][j], bands[3][j]
        inner, outer = jnp.where(even, last, first), jnp.where(even, first, last)
        tiles = [inner, edge, outer, bands[1][j], bands[2][j]]
        out_ref[pl.ds(dates * j, dates), :] = jnp.concatenate(tiles, axis=1).astype(BF16)


NEAR, FAR = 0, 1
OWN_TILES = ((0, 1, 3, 4), (1, 2, 3, 4))


def window_masks():
    lane = np.arange(LANES)
    sub, c = lane // 8 % 4, lane % 8
    band = np.where(c < 4, sub, (sub + 1) % 4)
    inner = np.where((c < 4) | (band == 0), lane // 32, (lane // 32 - 1) % 4)
    edge = (4 * band + inner, np.where(c < 4, 32 + c, c - 8))
    plain = [(4 * g + lane // 32, lane % 32) for g in range(4)]
    masks = np.zeros((2, 2, 4, 6, LANES), np.float32)
    for odd in range(2):
        own = [plain[0 if odd else 3], edge, plain[3 if odd else 0], plain[1], plain[2]]
        other = [plain[3 if odd else 0], edge, plain[0 if odd else 3]]
        for phase in (NEAR, FAR):
            y = 1 - odd if phase == NEAR else odd
            shift = 16 if y else -16
            halo = other[:2] if phase == NEAR else other[1:]
            tiles = [own[t] for t in OWN_TILES[phase]] + [(r + shift, k) for r, k in halo]
            for x in range(4):
                for t, (row, col) in enumerate(tiles):
                    inside = (row >= 8 * y - 3) & (row <= 8 * y + 11) & (col >= 8 * x - 3) & (col <= 8 * x + 11)
                    masks[odd, phase, x, t] = inside
    assert (masks.sum(axis=(3, 4)) == 225).all()
    return masks.reshape(2, 8, 6 * LANES)


def encode(value):
    value = value * 32768.0
    square = value * value
    fourth = square * square
    return fourth * square * (value * jnp.abs(value))


def decode(code):
    size = jnp.abs(code)
    root = lax.rsqrt(lax.rsqrt(jnp.maximum(size, 1.2e-38)))
    root = root * lax.rsqrt(root) * (1.0 / 32768.0)
    root = jnp.where(size == 0.0, 0.0, root)
    return jnp.where(code < 0.0, -root, root)


def matrices(rows):
    target, source = iota((rows // 2, rows), 0), iota((rows // 2, rows), 1)
    place = target // 4 * 8 + target % 4
    pick_re = (source == place).astype(F32)
    pick_im = (source == place + 4).astype(F32)
    target, source = iota((rows, rows), 0), iota((rows, rows), 1)
    first = target % 8 < 4
    turn = jnp.where(first & (source == target + 4), 1.0, 0.0) - jnp.where(~first & (source == target - 4), 1.0, 0.0)
    return jnp.concatenate([turn, pick_re, pick_im], axis=0).astype(BF16)


def views(samples):
    return jnp.dot(matrices(samples.shape[0]), samples, preferred_element_type=F32).astype(BF16)


def products(samples, view, masks):
    rows = samples.shape[0]
    dates = rows // 2
    left = jnp.concatenate([samples, view[:rows]], axis=1)
    right = jnp.concatenate([view[rows:rows + dates], view[rows + dates:]], axis=1)
    both = jnp.concatenate([right * jnp.concatenate([mask, mask], axis=1) for mask in masks], axis=0)
    return lax.dot_general(left, both, (((1,), (1,)), ((), ())), preferred_element_type=F32)


def chosen(array, which):
    return jnp.concatenate([array[:, LANES * t:LANES * (t + 1)] for t in which], axis=1)


def mask_pair(masks_ref, phase, half):
    odd = lax.axis_index("row") % 2
    return [masks_ref[odd, pl.ds(4 * phase + 2 * half + x, 1), :].astype(BF16) for x in range(2)]


def coded(sums, own, own_re):
    rows, dates = own.shape
    codes = []
    for x in range(2):
        part = sums[:, dates * x:dates * (x + 1)]
        power = jnp.sum(jnp.where(own_re, part, 0.0), axis=0, keepdims=True)
        scale = lax.rsqrt(power + 1e-06)
        own_scale = jnp.sum(jnp.where(own, scale, 0.0), axis=1, keepdims=True)
        codes.append(encode(part * own_scale * scale).reshape(rows // 8, 8, dates))
    return jnp.concatenate(codes, axis=1).astype(BF16)


def own_kernel(samples_ref, masks_ref, sums_ref, near_ref):
    near_ref[...] = samples_ref[:, :2 * LANES]
    width = len(OWN_TILES[NEAR]) * LANES
    samples = samples_ref[...]
    view = views(samples)
    for phase in (NEAR, FAR):
        for half in range(2):
            masks = [mask[:, :width] for mask in mask_pair(masks_ref, phase, half)]
            tiles = OWN_TILES[phase]
            sums_ref[2 * phase + half] = products(chosen(samples, tiles), chosen(view, tiles), masks)


def finish_kernel(sums_ref, near_ref, far_ref, masks_ref, out_ref):
    width = len(OWN_TILES[FAR]) * LANES
    rows = near_ref.shape[0]
    dates = rows // 2
    target, source = iota((rows, dates), 0), iota((rows, dates), 1)
    own = target // 8 * 4 + target % 4 == source
    own_re = own & (target % 8 < 4)
    halos = jnp.concatenate([near_ref[...], far_ref[...]], axis=1)
    halo_views = views(halos)
    for phase in (NEAR, FAR):
        part = slice(2 * LANES * phase, 2 * LANES * (phase + 1))
        for half in range(2):
            masks = [mask[:, width:] for mask in mask_pair(masks_ref, phase, half)]
            group = 2 * phase + half
            sums = sums_ref[group] + products(halos[:, part], halo_views[:, part], masks)
            out_ref[:, 16 * group:16 * (group + 1), :] = coded(sums, own, own_re)


def spread_kernel(codes_ref, out_ref, codes, results, sems):
    parts = codes_ref.shape[0] // 64
    dates = codes_ref.shape[1]
    odd = lax.axis_index("row") % 2
    codes[...] = codes_ref[...].astype(F32)
    source, target = iota((8 * parts, 8 * parts), 0), iota((8 * parts, 8 * parts), 1)
    cols = 4 * parts
    phase = (target // cols + odd + 1) % 2
    wanted = target % cols // 4 * 8 + phase * 4 + target % 4
    order = (source == wanted).astype(F32).astype(BF16)
    copies = []
    for k in range(8):
        block = codes[pl.ds(k, 8 * parts, stride=8), :].astype(BF16)
        moved = lax.dot_general(block, order, (((0,), (0,)), ((), ())), preferred_element_type=F32)
        moved = decode(moved)
        for y in range(2):
            results[k, pl.ds(y, dates, stride=2), :] = moved[:, cols * y:cols * (y + 1)]
        copies.append(pltpu.make_async_copy(results.at[k], out_ref.at[k], sems.at[k]))
        copies[k].start()
    for copy in copies:
        copy.wait()


VMEM = pl.BlockSpec(memory_space=pltpu.VMEM)
HBM = pl.BlockSpec(memory_space=pltpu.HBM)


def call(kernel, name, shapes, scratch=(), flops=0, outputs=VMEM):
    def run(*arrays):
        return pl.pallas_call(
            kernel,
            out_shape=[jax.ShapeDtypeStruct(*shape) for shape in shapes],
            in_specs=[VMEM] * len(arrays),
            out_specs=[outputs] * len(shapes),
            scratch_shapes=list(scratch),
            compiler_params=pltpu.CompilerParams(vmem_limit_bytes=32 * 1024 * 1024),
            cost_estimate=pl.CostEstimate(flops=flops, bytes_accessed=1 << 20, transcendentals=0),
            name=name,
        )(*arrays)

    return run


def on_device(slc):
    dates = slc.shape[1]
    rows, cols = slc.shape[2], slc.shape[3]
    groups = lax.axis_size("row")
    parts = lax.axis_size("date")
    total = parts * dates
    width = TILES * LANES
    own = slc.reshape(2 * dates * rows, cols)
    lines = parts * 2 * dates
    chunks = cols // LANES
    (packed,) = call(pack_kernel, "pack", [((lines, width), BF16)])(own)

    def exchange(array):
        blocks = array.reshape(parts, array.size // parts // array.shape[-1], array.shape[-1])
        return lax.all_to_all(blocks, "date", 0, 0, tiled=True).reshape(-1, array.shape[-1])

    def swapped(array, first):
        pairs = [(i, i + 1) for i in range(first, groups - 1, 2)]
        return lax.ppermute(array, "row", pairs + [(j, i) for i, j in pairs])

    samples = exchange(packed)
    far = swapped(samples[:, LANES:3 * LANES], 1)
    masks = jnp.asarray(window_masks())
    sums, message = call(
        own_kernel, "own", [((4, lines, 2 * total), F32), ((lines, 2 * LANES), BF16)], flops=1 << 30
    )(samples, masks)
    near = swapped(message, 0)
    (codes,) = call(finish_kernel, "finish", [((parts, 64, total), BF16)], flops=1 << 30)(sums, near, far, masks)
    codes = exchange(codes)
    (out,) = call(
        spread_kernel, "spread", [((2 * dates, 2 * total, chunks * 16), F32)],
        [
            pltpu.VMEM((parts * 64, total), F32),
            pltpu.VMEM((2 * dates, 2 * total, chunks * 16), F32),
            pltpu.SemaphoreType.DMA((2 * dates,)),
        ],
        outputs=HBM,
    )(codes)
    return out.reshape(2, dates, total, rows // 8, cols // 8)


def solution(mesh):
    return jax.shard_map(
        on_device,
        mesh=mesh,
        in_specs=(P(None, "date", "row", None),),
        out_specs=P(None, "date", None, "row", None),
        check_vma=False,
    )
```

time: 320 us -> 89.8 us (0.28)
  the two profiles are of different devices: /device:TPU:2 before, /device:TPU:35 now
where the time goes in v1:
time: 89.8 us; the launch traced here: 89.5 us
  blocking collectives  73.7 us (82%)
  starting transfers between devices  9.45 us (11%)
  Pallas kernels  4.06 us (5%)
  waiting for transfers between devices  1.31 us (1%)
  local copies, waits for them, and re-layouts  0.96 us (1%)
    all_to_all x2, blocking collectives, exchange(): lax.all_to_all(blocks, 'date', 0, 0, tiled=True)  73.7 us
    ppermute x2, starting transfers between devices, swapped(): return lax.ppermute(array, 'row', pairs + [(j, i) for i, j in pairs])  9.45 us
    pallas_call x4, Pallas kernels, run(): pl.pallas_call(kernel, out_shape=[jax.ShapeDtypeStruct(*shape) for shape...  4.06 us
  transfers between devices with their start and end apart: 2, of which 2 were waited for; matrix products, arithmetic and copies ran while one was open for 0% of the time, Pallas kernels for 1%

profile of v1, /device:TPU:35, one launch (start us, length us, event | category | flops | bytes accessed | tf_op | source)
XLA Modules:
  0.0 89.5 jit_solution(5872915118765154912)
XLA Ops:
  0.0 0.0 copy-start
  0.0 0.9 %copy-done = bf16[2,4,16,1024]{3,2,1,0:T(8,128)(2,1)S(1)} copy-done((bf16[2,4,16,1024]{3,2,1,0:T(8,128)(2,1)S(1)}, bf16[2,4,16,1024]{3,2,1,0:T(8,128)(2,1)}, u32[]{:S(2)}) %copy-start) | copy-done | bytes 262168
  1.0 0.4 pack.1
  1.4 37.6 %all_to_all.10 = bf16[32,8,640]{2,1,0:T(8,128)(2,1)S(1)} all-to-all(bf16[32,8,640]{2,1,0:T(8,128)(2,1)S(1)} %bitcast.6), channel_id=1, replica_groups=mesh['date'=32,'row'=16] {'date'}, dimensions={0} | all-to-all | bytes 655360 | tf_op jit(solution)/shard_map/all_to_all | solution.py:244
  39.0 0.0 copy-start.1
  39.0 7.5 %collective-permute-start.1 = (bf16[256,256]{1,0:T(8,128)(2,1)S(1)}, bf16[256,256]{1,0:T(8,128)(2,1)S(1)}, u32[]{:S(2)}, u32[]{:S(2)}) collective-permute-start(bf16[256,256]{1,0:T(8,128)(2,1)S(1)} %slice.4), channel_id=1, source_target_pairs={{1,2},{3,4},{5,6},{7,8},{9,10},{11,12},{13,14},{2,1},{4,3},{6,5},{... | collective-permute-start | bytes 393224 | tf_op jit(solution)/shard_map/ppermute | solution.py:248
  46.5 0.0 copy-done.1
  46.6 1.0 %own.1 = (f32[4,256,256]{2,1,0:T(8,128)S(1)}, bf16[256,256]{1,0:T(8,128)(2,1)S(1)}) custom-call(bf16[256,640]{1,0:T(8,128)(2,1)S(1)} %bitcast.8, f32[2,8,768]{2,1,0:T(8,128)S(1)} %copy-done.1), custom_call_target="tpu_custom_call" | custom-call | flops 1073741824 | bytes 1048576 | tf_op jit(solution)/shard_map/own/pallas_call | solution.py:216
  47.6 1.9 %collective-permute-start = (bf16[256,256]{1,0:T(8,128)(2,1)S(1)}, bf16[256,256]{1,0:T(8,128)(2,1)S(1)}, u32[]{:S(2)}, u32[]{:S(2)}) collective-permute-start(bf16[256,256]{1,0:T(8,128)(2,1)S(1)} %get-tuple-element.8), channel_id=1, source_target_pairs={{0,1},{2,3},{4,5},{6,7},{8,9},{10,11},{12,13},{14,15},{1,0},{3,2},... | collective-permute-start | bytes 393224 | tf_op jit(solution)/shard_map/ppermute | solution.py:248
  49.5 1.1 %collective-permute-done.1.far_ref = bf16[256,256]{1,0:T(8,128)(2,1)S(1)} collective-permute-done((bf16[256,256]{1,0:T(8,128)(2,1)S(1)}, bf16[256,256]{1,0:T(8,128)(2,1)S(1)}, u32[]{:S(2)}, u32[]{:S(2)}) %collective-permute-start.1) | collective-permute-done | bytes 131104 | tf_op jit(solution)/shard_map/ppermute | solution.py:248
  50.6 0.2 collective-permute-done.near_ref
  50.8 1.1 %finish.1 = bf16[32,64,128]{2,1,0:T(8,128)(2,1)S(1)} custom-call(f32[4,256,256]{2,1,0:T(8,128)S(1)} %get-tuple-element.7.sums_ref, bf16[256,256]{1,0:T(8,128)(2,1)S(1)} %collective-permute-done.near_ref, bf16[256,256]{1,0:T(8,128)(2,1)S(1)} %collective-permute-done.1.far_ref, f32[2,8,768]{2,1,0:T(8,128)S(1)} %copy-done.1), custom_call_target="tpu_custom_call" | custom-call | flops 1073741824 | bytes 1048576 | tf_op jit(solution)/shard_map/finish/pallas_call | solution.py:216
  51.9 36.1 %all_to_all.11 = bf16[32,64,128]{2,1,0:T(8,128)(2,1)S(1)} all-to-all(bf16[32,64,128]{2,1,0:T(8,128)(2,1)S(1)} %finish.1), channel_id=1, replica_groups=mesh['date'=32,'row'=16] {'date'}, dimensions={0} | all-to-all | bytes 1048576 | tf_op jit(solution)/shard_map/all_to_all | solution.py:244
  88.0 1.5 %spread.1 = f32[8,256,128]{2,1,0:T(8,128)} custom-call(bf16[2048,128]{1,0:T(8,128)(2,1)S(1)} %bitcast.5), custom_call_target="tpu_custom_call" | custom-call | bytes 1048576 | tf_op jit(solution)/shard_map/spread/pallas_call | solution.py:216
  (1 shorter events, 0.0 us)
Async XLA Ops:
  0.0 0.9 %copy-start = (bf16[2,4,16,1024]{3,2,1,0:T(8,128)(2,1)S(1)}, bf16[2,4,16,1024]{3,2,1,0:T(8,128)(2,1)}, u32[]{:S(2)}) copy-start(bf16[2,4,16,1024]{3,2,1,0:T(8,128)(2,1)} %param.2) | copy-start | bytes 786436
  39.0 7.6 %copy-start.1 = (f32[2,8,768]{2,1,0:T(8,128)S(1)}, f32[2,8,768]{2,1,0:T(8,128)}, u32[]{:S(2)}) copy-start(f32[2,8,768]{2,1,0:T(8,128)} %constant.2.clone.masks_ref) | copy-start | bytes 147460
  39.0 11.6 %collective-permute-start.1 = (bf16[256,256]{1,0:T(8,128)(2,1)S(1)}, bf16[256,256]{1,0:T(8,128)(2,1)S(1)}, u32[]{:S(2)}, u32[]{:S(2)}) collective-permute-start(bf16[256,256]{1,0:T(8,128)(2,1)S(1)} %slice.4), channel_id=1, source_target_pairs={{1,2},{3,4},{5,6},{7,8},{9,10},{11,12},{13,14},{2,1},{4,3},{6,5},{... | collective-permute-start | bytes 393224 | tf_op jit(solution)/shard_map/ppermute | solution.py:248
  47.6 3.2 %collective-permute-start = (bf16[256,256]{1,0:T(8,128)(2,1)S(1)}, bf16[256,256]{1,0:T(8,128)(2,1)S(1)}, u32[]{:S(2)}, u32[]{:S(2)}) collective-permute-start(bf16[256,256]{1,0:T(8,128)(2,1)S(1)} %get-tuple-element.8), channel_id=1, source_target_pairs={{0,1},{2,3},{4,5},{6,7},{8,9},{10,11},{12,13},{14,15},{1,0},{3,2},... | collective-permute-start | bytes 393224 | tf_op jit(solution)/shard_map/ppermute | solution.py:248

commit v2 on v1

--- a/solution.py
+++ b/solution.py
@@ -30,6 +30,15 @@
             vregs[i + step] = jnp.where(upper, b, pltpu.roll(a, LANES - shift, 1))
         step *= 2
     return vregs
+
+
+def folded(parts):
+    lane = iota(parts[0].shape, 1)
+    slot = jnp.where(lane % 8 < 4, lane // 8 % 4, (lane // 8 + 1) % 4)
+    whole = parts[0]
+    for q in range(1, 4):
+        whole = jnp.where(slot == q, pltpu.roll(parts[q], 8 * q, 1), whole)
+    return whole
 
 
 def pack_kernel(own_ref, out_ref):
@@ -51,17 +60,18 @@
                 bands[g] += butterfly(rows, 32, lane)
     zero = jnp.zeros((dates, LANES), F32)
     low = lane % 8 < 4
-    slot = jnp.where(low, lane // 8 % 4, (lane // 8 + 1) % 4)
     for j in range(parts):
-        edge = None
+        edges = []
         for g in range(4):
             after = zero if j == parts - 1 else bands[g][j + 1]
             before = zero if j == 0 else bands[g][j - 1]
-            both = jnp.where(low, after, before)
-            both = pltpu.roll(both, 8 * g, 1) if g else both
-            edge = both if edge is None else jnp.where(slot == g, both, edge)
-        first, last = bands[0][j], bands[3][j]
-        inner, outer = jnp.where(even, last, first), jnp.where(even, first, last)
+            edges.append(jnp.where(low, after, before))
+
+        def sides(first, last):
+            return jnp.where(even, first, last), jnp.where(even, last, first)
+
+        outer, inner = sides(bands[0][j], bands[3][j])
+        edge = folded([*sides(edges[0], edges[3]), edges[1], edges[2]])
         tiles = [inner, edge, outer, bands[1][j], bands[2][j]]
         out_ref[pl.ds(dates * j, dates), :] = jnp.concatenate(tiles, axis=1).astype(BF16)
 
@@ -73,14 +83,17 @@
 def window_masks():
     lane = np.arange(LANES)
     sub, c = lane // 8 % 4, lane % 8
-    band = np.where(c < 4, sub, (sub + 1) % 4)
-    inner = np.where((c < 4) | (band == 0), lane // 32, (lane // 32 - 1) % 4)
-    edge = (4 * band + inner, np.where(c < 4, 32 + c, c - 8))
+    role = np.where(c < 4, sub, (sub + 1) % 4)
+    inner = np.where((c < 4) | (role == 0), lane // 32, (lane // 32 - 1) % 4)
+    edges = []
+    for odd in range(2):
+        band = np.array([3, 0, 1, 2] if odd else [0, 3, 1, 2])[role]
+        edges.append((4 * band + inner, np.where(c < 4, 32 + c, c - 8)))
     plain = [(4 * g + lane // 32, lane % 32) for g in range(4)]
     masks = np.zeros((2, 2, 4, 6, LANES), np.float32)
     for odd in range(2):
-        own = [plain[0 if odd else 3], edge, plain[3 if odd else 0], plain[1], plain[2]]
-        other = [plain[3 if odd else 0], edge, plain[0 if odd else 3]]
+        own = [plain[0 if odd else 3], edges[odd], plain[3 if odd else 0], plain[1], plain[2]]
+        other = [plain[3 if odd else 0], edges[1 - odd], plain[0 if odd else 3]]
         for phase in (NEAR, FAR):
             y = 1 - odd if phase == NEAR else odd
             shift = 16 if y else -16
@@ -154,8 +167,24 @@
     return jnp.concatenate(codes, axis=1).astype(BF16)
 
 
-def own_kernel(samples_ref, masks_ref, sums_ref, near_ref):
-    near_ref[...] = samples_ref[:, :2 * LANES]
+def message_kernel(samples_ref, far_ref, near_ref):
+    rows = samples_ref.shape[0]
+    edge = samples_ref[:, LANES:2 * LANES].astype(F32)
+    for out_ref, tile, lanes in ((far_ref, 2, 0), (near_ref, 0, 8)):
+        out_ref[:rows] = samples_ref[:, LANES * tile:LANES * (tile + 1)]
+        parts = [edge[rows // 4 * q:rows // 4 * (q + 1)] for q in range(4)]
+        parts = [pltpu.roll(part, LANES - lanes, 1) if lanes else part for part in parts]
+        out_ref[rows:] = folded(parts).astype(BF16)
+
+
+def unfolded(message, lanes):
+    rows = message.shape[0] // 5 * 4
+    edge = message[rows:].astype(F32)
+    turned = [pltpu.roll(edge, (LANES - 8 * q + lanes) % LANES, 1) for q in range(4)]
+    return message[:rows], jnp.concatenate(turned, axis=0).astype(BF16)
+
+
+def own_kernel(samples_ref, masks_ref, sums_ref):
     width = len(OWN_TILES[NEAR]) * LANES
     samples = samples_ref[...]
     view = views(samples)
@@ -166,14 +195,16 @@
             sums_ref[2 * phase + half] = products(chosen(samples, tiles), chosen(view, tiles), masks)
 
 
-def finish_kernel(sums_ref, near_ref, far_ref, masks_ref, out_ref):
+def finish_kernel(sums_ref, far_ref, near_ref, masks_ref, out_ref):
     width = len(OWN_TILES[FAR]) * LANES
-    rows = near_ref.shape[0]
+    rows = near_ref.shape[0] // 5 * 4
     dates = rows // 2
     target, source = iota((rows, dates), 0), iota((rows, dates), 1)
     own = target // 8 * 4 + target % 4 == source
     own_re = own & (target % 8 < 4)
-    halos = jnp.concatenate([near_ref[...], far_ref[...]], axis=1)
+    inner, inner_edge = unfolded(near_ref[...], 8)
+    outer, outer_edge = unfolded(far_ref[...], 0)
+    halos = jnp.concatenate([inner, inner_edge, outer_edge, outer], axis=1)
     halo_views = views(halos)
     for phase in (NEAR, FAR):
         part = slice(2 * LANES * phase, 2 * LANES * (phase + 1))
@@ -248,13 +279,13 @@
         return lax.ppermute(array, "row", pairs + [(j, i) for i, j in pairs])
 
     samples = exchange(packed)
-    far = swapped(samples[:, LANES:3 * LANES], 1)
+    far, near = call(
+        message_kernel, "message", [((lines // 4 * 5, LANES), BF16)] * 2
+    )(samples)
+    far, near = swapped(far, 1), swapped(near, 0)
     masks = jnp.asarray(window_masks())
-    sums, message = call(
-        own_kernel, "own", [((4, lines, 2 * total), F32), ((lines, 2 * LANES), BF16)], flops=1 << 30
-    )(samples, masks)
-    near = swapped(message, 0)
-    (codes,) = call(finish_kernel, "finish", [((parts, 64, total), BF16)], flops=1 << 30)(sums, near, far, masks)
+    (sums,) = call(own_kernel, "own", [((4, lines, 2 * total), F32)], flops=1 << 30)(samples, masks)
+    (codes,) = call(finish_kernel, "finish", [((parts, 64, total), BF16)], flops=1 << 30)(sums, far, near, masks)
     codes = exchange(codes)
     (out,) = call(
         spread_kernel, "spread", [((2 * dates, 2 * total, chunks * 16), F32)],

time: 89.8 us -> 89.3 us (level)
  the two profiles are of different devices: /device:TPU:35 before, /device:TPU:36 now
where the time goes in v2:
time: 89.3 us; the launch traced here: 89.1 us
  blocking collectives  76.6 us (86%)
  starting transfers between devices  6.84 us (8%)
  Pallas kernels  4.31 us (5%)
  local copies, waits for them, and re-layouts  0.95 us (1%)
    all_to_all x2, blocking collectives, exchange(): lax.all_to_all(blocks, 'date', 0, 0, tiled=True)  76.6 us
    ppermute x2, starting transfers between devices, swapped(): return lax.ppermute(array, 'row', pairs + [(j, i) for i, j in pairs])  6.84 us
    pallas_call x5, Pallas kernels, run(): pl.pallas_call(kernel, out_shape=[jax.ShapeDtypeStruct(*shape) for shape...  4.31 us
  transfers between devices with their start and end apart: 2, of which 1 were waited for; matrix products, arithmetic and copies ran while one was open for 0% of the time, Pallas kernels for 1%

profile of v2, /device:TPU:36, one launch (start us, length us, event | category | flops | bytes accessed | tf_op | source)
XLA Modules:
  0.0 89.1 jit_solution(5422401159590460898)
XLA Ops:
  0.0 0.0 copy-start
  0.0 0.9 %copy-done = bf16[2,4,16,1024]{3,2,1,0:T(8,128)(2,1)S(1)} copy-done((bf16[2,4,16,1024]{3,2,1,0:T(8,128)(2,1)S(1)}, bf16[2,4,16,1024]{3,2,1,0:T(8,128)(2,1)}, u32[]{:S(2)}) %copy-start) | copy-done | bytes 262168
  1.0 0.5 pack.1
  1.4 40.0 %all_to_all.10 = bf16[32,8,640]{2,1,0:T(8,128)(2,1)S(1)} all-to-all(bf16[32,8,640]{2,1,0:T(8,128)(2,1)S(1)} %bitcast.8), channel_id=1, replica_groups=mesh['date'=32,'row'=16] {'date'}, dimensions={0} | all-to-all | bytes 655360 | tf_op jit(solution)/shard_map/all_to_all | solution.py:275
  41.5 0.0 copy-start.1
  41.5 0.2 message.1
  41.6 1.9 %collective-permute-start = (bf16[320,128]{1,0:T(8,128)(2,1)S(1)}, bf16[320,128]{1,0:T(8,128)(2,1)S(1)}, u32[]{:S(2)}, u32[]{:S(2)}) collective-permute-start(bf16[320,128]{1,0:T(8,128)(2,1)S(1)} %get-tuple-element.7), channel_id=1, source_target_pairs={{1,2},{3,4},{5,6},{7,8},{9,10},{11,12},{13,14},{2,1},{4,3},{6,5},{... | collective-permute-start | bytes 245768 | tf_op jit(solution)/shard_map/ppermute | solution.py:279
  43.6 4.9 %collective-permute-start.1 = (bf16[320,128]{1,0:T(8,128)(2,1)S(1)}, bf16[320,128]{1,0:T(8,128)(2,1)S(1)}, u32[]{:S(2)}, u32[]{:S(2)}) collective-permute-start(bf16[320,128]{1,0:T(8,128)(2,1)S(1)} %get-tuple-element.8), channel_id=1, source_target_pairs={{0,1},{2,3},{4,5},{6,7},{8,9},{10,11},{12,13},{14,15},{1,0},{3,2},... | collective-permute-start | bytes 245768 | tf_op jit(solution)/shard_map/ppermute | solution.py:279
  48.5 0.0 copy-done.1
  48.5 1.0 %own.1.sums_ref = f32[4,256,256]{2,1,0:T(8,128)S(1)} custom-call(bf16[256,640]{1,0:T(8,128)(2,1)S(1)} %bitcast.7, f32[2,8,768]{2,1,0:T(8,128)S(1)} %copy-done.1), custom_call_target="tpu_custom_call" | custom-call | flops 1073741824 | bytes 1048576 | tf_op jit(solution)/shard_map/own/pallas_call | solution.py:247
  49.5 0.3 collective-permute-done.far_ref
  49.8 0.0 collective-permute-done.1.near_ref
  49.8 1.2 %finish.1 = bf16[32,64,128]{2,1,0:T(8,128)(2,1)S(1)} custom-call(f32[4,256,256]{2,1,0:T(8,128)S(1)} %own.1.sums_ref, bf16[320,128]{1,0:T(8,128)(2,1)S(1)} %collective-permute-done.far_ref, bf16[320,128]{1,0:T(8,128)(2,1)S(1)} %collective-permute-done.1.near_ref, f32[2,8,768]{2,1,0:T(8,128)S(1)} %copy-done.1), custom_call_target="tpu_custom_call" | custom-call | flops 1073741824 | bytes 1048576 | tf_op jit(solution)/shard_map/finish/pallas_call | solution.py:247
  51.0 36.6 %all_to_all.11 = bf16[32,64,128]{2,1,0:T(8,128)(2,1)S(1)} all-to-all(bf16[32,64,128]{2,1,0:T(8,128)(2,1)S(1)} %finish.1), channel_id=1, replica_groups=mesh['date'=32,'row'=16] {'date'}, dimensions={0} | all-to-all | bytes 1048576 | tf_op jit(solution)/shard_map/all_to_all | solution.py:275
  87.5 1.5 %spread.1 = f32[8,256,128]{2,1,0:T(8,128)} custom-call(bf16[2048,128]{1,0:T(8,128)(2,1)S(1)} %bitcast.5), custom_call_target="tpu_custom_call" | custom-call | bytes 1048576 | tf_op jit(solution)/shard_map/spread/pallas_call | solution.py:247
Async XLA Ops:
  0.0 0.9 %copy-start = (bf16[2,4,16,1024]{3,2,1,0:T(8,128)(2,1)S(1)}, bf16[2,4,16,1024]{3,2,1,0:T(8,128)(2,1)}, u32[]{:S(2)}) copy-start(bf16[2,4,16,1024]{3,2,1,0:T(8,128)(2,1)} %param.2) | copy-start | bytes 786436
  41.5 7.0 %copy-start.1 = (f32[2,8,768]{2,1,0:T(8,128)S(1)}, f32[2,8,768]{2,1,0:T(8,128)}, u32[]{:S(2)}) copy-start(f32[2,8,768]{2,1,0:T(8,128)} %constant.2.clone.masks_ref) | copy-start | bytes 147460
  41.6 8.2 %collective-permute-start = (bf16[320,128]{1,0:T(8,128)(2,1)S(1)}, bf16[320,128]{1,0:T(8,128)(2,1)S(1)}, u32[]{:S(2)}, u32[]{:S(2)}) collective-permute-start(bf16[320,128]{1,0:T(8,128)(2,1)S(1)} %get-tuple-element.7), channel_id=1, source_target_pairs={{1,2},{3,4},{5,6},{7,8},{9,10},{11,12},{13,14},{2,1},{4,3},{6,5},{... | collective-permute-start | bytes 245768 | tf_op jit(solution)/shard_map/ppermute | solution.py:279
  43.6 6.2 %collective-permute-start.1 = (bf16[320,128]{1,0:T(8,128)(2,1)S(1)}, bf16[320,128]{1,0:T(8,128)(2,1)S(1)}, u32[]{:S(2)}, u32[]{:S(2)}) collective-permute-start(bf16[320,128]{1,0:T(8,128)(2,1)S(1)} %get-tuple-element.8), channel_id=1, source_target_pairs={{0,1},{2,3},{4,5},{6,7},{8,9},{10,11},{12,13},{14,15},{1,0},{3,2},... | collective-permute-start | bytes 245768 | tf_op jit(solution)/shard_map/ppermute | solution.py:279

commit v3 on v2

--- a/solution.py
+++ b/solution.py
@@ -108,16 +108,15 @@
 
 
 def encode(value):
-    value = value * 32768.0
+    value = value * 131072.0
     square = value * value
     fourth = square * square
-    return fourth * square * (value * jnp.abs(value))
+    return fourth * square * value
 
 
 def decode(code):
     size = jnp.abs(code)
-    root = lax.rsqrt(lax.rsqrt(jnp.maximum(size, 1.2e-38)))
-    root = root * lax.rsqrt(root) * (1.0 / 32768.0)
+    root = lax.exp2(jnp.log(jnp.maximum(size, 1.2e-38)) * (1.0 / (7.0 * np.log(2.0))) - 17.0)
     root = jnp.where(size == 0.0, 0.0, root)
     return jnp.where(code < 0.0, -root, root)
 

time: 89.3 us -> 89.3 us (level)
  no operation moved by 1% of the time
where the time goes in v3:
time: 89.3 us; the launch traced here: 89 us
  blocking collectives  76.6 us (86%)
  starting transfers between devices  6.84 us (8%)
  Pallas kernels  4.25 us (5%)
  local copies, waits for them, and re-layouts  0.95 us (1%)
    all_to_all x2, blocking collectives, exchange(): lax.all_to_all(blocks, 'date', 0, 0, tiled=True)  76.6 us
    ppermute x2, starting transfers between devices, swapped(): return lax.ppermute(array, 'row', pairs + [(j, i) for i, j in pairs])  6.84 us
    pallas_call x5, Pallas kernels, run(): pl.pallas_call(kernel, out_shape=[jax.ShapeDtypeStruct(*shape) for shape...  4.25 us
  transfers between devices with their start and end apart: 2, of which 1 were waited for; matrix products, arithmetic and copies ran while one was open for 0% of the time, Pallas kernels for 1%

profile of v3, /device:TPU:36, one launch (start us, length us, event | category | flops | bytes accessed | tf_op | source)
XLA Modules:
  0.0 89.0 jit_solution(10280296046648858828)
XLA Ops:
  0.0 0.0 copy-start
  0.0 0.9 %copy-done = bf16[2,4,16,1024]{3,2,1,0:T(8,128)(2,1)S(1)} copy-done((bf16[2,4,16,1024]{3,2,1,0:T(8,128)(2,1)S(1)}, bf16[2,4,16,1024]{3,2,1,0:T(8,128)(2,1)}, u32[]{:S(2)}) %copy-start) | copy-done | bytes 262168
  1.0 0.5 pack.1
  1.4 40.0 %all_to_all.10 = bf16[32,8,640]{2,1,0:T(8,128)(2,1)S(1)} all-to-all(bf16[32,8,640]{2,1,0:T(8,128)(2,1)S(1)} %bitcast.8), channel_id=1, replica_groups=mesh['date'=32,'row'=16] {'date'}, dimensions={0} | all-to-all | bytes 655360 | tf_op jit(solution)/shard_map/all_to_all | solution.py:274
  41.5 0.0 copy-start.1
  41.5 0.2 message.1
  41.6 1.9 %collective-permute-start = (bf16[320,128]{1,0:T(8,128)(2,1)S(1)}, bf16[320,128]{1,0:T(8,128)(2,1)S(1)}, u32[]{:S(2)}, u32[]{:S(2)}) collective-permute-start(bf16[320,128]{1,0:T(8,128)(2,1)S(1)} %get-tuple-element.7), channel_id=1, source_target_pairs={{1,2},{3,4},{5,6},{7,8},{9,10},{11,12},{13,14},{2,1},{4,3},{6,5},{... | collective-permute-start | bytes 245768 | tf_op jit(solution)/shard_map/ppermute | solution.py:278
  43.6 4.9 %collective-permute-start.1 = (bf16[320,128]{1,0:T(8,128)(2,1)S(1)}, bf16[320,128]{1,0:T(8,128)(2,1)S(1)}, u32[]{:S(2)}, u32[]{:S(2)}) collective-permute-start(bf16[320,128]{1,0:T(8,128)(2,1)S(1)} %get-tuple-element.8), channel_id=1, source_target_pairs={{0,1},{2,3},{4,5},{6,7},{8,9},{10,11},{12,13},{14,15},{1,0},{3,2},... | collective-permute-start | bytes 245768 | tf_op jit(solution)/shard_map/ppermute | solution.py:278
  48.5 0.0 copy-done.1
  48.5 1.0 %own.1.sums_ref = f32[4,256,256]{2,1,0:T(8,128)S(1)} custom-call(bf16[256,640]{1,0:T(8,128)(2,1)S(1)} %bitcast.7, f32[2,8,768]{2,1,0:T(8,128)S(1)} %copy-done.1), custom_call_target="tpu_custom_call" | custom-call | flops 1073741824 | bytes 1048576 | tf_op jit(solution)/shard_map/own/pallas_call | solution.py:246
  49.5 0.3 collective-permute-done.far_ref
  49.8 0.0 collective-permute-done.1.near_ref
  49.8 1.1 %finish.1 = bf16[32,64,128]{2,1,0:T(8,128)(2,1)S(1)} custom-call(f32[4,256,256]{2,1,0:T(8,128)S(1)} %own.1.sums_ref, bf16[320,128]{1,0:T(8,128)(2,1)S(1)} %collective-permute-done.far_ref, bf16[320,128]{1,0:T(8,128)(2,1)S(1)} %collective-permute-done.1.near_ref, f32[2,8,768]{2,1,0:T(8,128)S(1)} %copy-done.1), custom_call_target="tpu_custom_call" | custom-call | flops 1073741824 | bytes 1048576 | tf_op jit(solution)/shard_map/finish/pallas_call | solution.py:246
  50.9 36.6 %all_to_all.11 = bf16[32,64,128]{2,1,0:T(8,128)(2,1)S(1)} all-to-all(bf16[32,64,128]{2,1,0:T(8,128)(2,1)S(1)} %finish.1), channel_id=1, replica_groups=mesh['date'=32,'row'=16] {'date'}, dimensions={0} | all-to-all | bytes 1048576 | tf_op jit(solution)/shard_map/all_to_all | solution.py:274
  87.5 1.5 %spread.1 = f32[8,256,128]{2,1,0:T(8,128)} custom-call(bf16[2048,128]{1,0:T(8,128)(2,1)S(1)} %bitcast.5), custom_call_target="tpu_custom_call" | custom-call | bytes 1048576 | tf_op jit(solution)/shard_map/spread/pallas_call | solution.py:246
Async XLA Ops:
  0.0 0.9 %copy-start = (bf16[2,4,16,1024]{3,2,1,0:T(8,128)(2,1)S(1)}, bf16[2,4,16,1024]{3,2,1,0:T(8,128)(2,1)}, u32[]{:S(2)}) copy-start(bf16[2,4,16,1024]{3,2,1,0:T(8,128)(2,1)} %param.2) | copy-start | bytes 786436
  41.5 7.0 %copy-start.1 = (f32[2,8,768]{2,1,0:T(8,128)S(1)}, f32[2,8,768]{2,1,0:T(8,128)}, u32[]{:S(2)}) copy-start(f32[2,8,768]{2,1,0:T(8,128)} %constant.2.clone.masks_ref) | copy-start | bytes 147460
  41.6 8.2 %collective-permute-start = (bf16[320,128]{1,0:T(8,128)(2,1)S(1)}, bf16[320,128]{1,0:T(8,128)(2,1)S(1)}, u32[]{:S(2)}, u32[]{:S(2)}) collective-permute-start(bf16[320,128]{1,0:T(8,128)(2,1)S(1)} %get-tuple-element.7), channel_id=1, source_target_pairs={{1,2},{3,4},{5,6},{7,8},{9,10},{11,12},{13,14},{2,1},{4,3},{6,5},{... | collective-permute-start | bytes 245768 | tf_op jit(solution)/shard_map/ppermute | solution.py:278
  43.6 6.2 %collective-permute-start.1 = (bf16[320,128]{1,0:T(8,128)(2,1)S(1)}, bf16[320,128]{1,0:T(8,128)(2,1)S(1)}, u32[]{:S(2)}, u32[]{:S(2)}) collective-permute-start(bf16[320,128]{1,0:T(8,128)(2,1)S(1)} %get-tuple-element.8), channel_id=1, source_target_pairs={{0,1},{2,3},{4,5},{6,7},{8,9},{10,11},{12,13},{14,15},{1,0},{3,2},... | collective-permute-start | bytes 245768 | tf_op jit(solution)/shard_map/ppermute | solution.py:278

commit v4 on v3

--- a/solution.py
+++ b/solution.py
@@ -231,8 +231,10 @@
         moved = decode(moved)
         for y in range(2):
             results[k, pl.ds(y, dates, stride=2), :] = moved[:, cols * y:cols * (y + 1)]
-        copies.append(pltpu.make_async_copy(results.at[k], out_ref.at[k], sems.at[k]))
-        copies[k].start()
+        if k % 2:
+            pair = pl.ds(k - 1, 2)
+            copies.append(pltpu.make_async_copy(results.at[pair], out_ref.at[pair], sems.at[k // 2]))
+            copies[-1].start()
     for copy in copies:
         copy.wait()
 
@@ -291,7 +293,7 @@
         [
             pltpu.VMEM((parts * 64, total), F32),
             pltpu.VMEM((2 * dates, 2 * total, chunks * 16), F32),
-            pltpu.SemaphoreType.DMA((2 * dates,)),
+            pltpu.SemaphoreType.DMA((dates,)),
         ],
         outputs=HBM,
     )(codes)

time: 89.3 us -> 89.3 us (level)
  no operation moved by 1% of the time
where the time goes in v4:
time: 89.3 us; the launch traced here: 89 us
  blocking collectives  76.6 us (86%)
  starting transfers between devices  6.84 us (8%)
  Pallas kernels  4.22 us (5%)
  local copies, waits for them, and re-layouts  0.95 us (1%)
    all_to_all x2, blocking collectives, exchange(): lax.all_to_all(blocks, 'date', 0, 0, tiled=True)  76.6 us
    ppermute x2, starting transfers between devices, swapped(): return lax.ppermute(array, 'row', pairs + [(j, i) for i, j in pairs])  6.84 us
    pallas_call x5, Pallas kernels, run(): pl.pallas_call(kernel, out_shape=[jax.ShapeDtypeStruct(*shape) for shape...  4.22 us
  transfers between devices with their start and end apart: 2, of which 1 were waited for; matrix products, arithmetic and copies ran while one was open for 0% of the time, Pallas kernels for 1%

profile of v4, /device:TPU:36, one launch (start us, length us, event | category | flops | bytes accessed | tf_op | source)
XLA Modules:
  0.0 89.0 jit_solution(18034276710410015183)
XLA Ops:
  0.0 0.0 copy-start
  0.0 0.9 %copy-done = bf16[2,4,16,1024]{3,2,1,0:T(8,128)(2,1)S(1)} copy-done((bf16[2,4,16,1024]{3,2,1,0:T(8,128)(2,1)S(1)}, bf16[2,4,16,1024]{3,2,1,0:T(8,128)(2,1)}, u32[]{:S(2)}) %copy-start) | copy-done | bytes 262168
  1.0 0.5 pack.1
  1.4 40.0 %all_to_all.10 = bf16[32,8,640]{2,1,0:T(8,128)(2,1)S(1)} all-to-all(bf16[32,8,640]{2,1,0:T(8,128)(2,1)S(1)} %bitcast.8), channel_id=1, replica_groups=mesh['date'=32,'row'=16] {'date'}, dimensions={0} | all-to-all | bytes 655360 | tf_op jit(solution)/shard_map/all_to_all | solution.py:276
  41.5 0.0 copy-start.1
  41.5 0.2 message.1
  41.6 1.9 %collective-permute-start = (bf16[320,128]{1,0:T(8,128)(2,1)S(1)}, bf16[320,128]{1,0:T(8,128)(2,1)S(1)}, u32[]{:S(2)}, u32[]{:S(2)}) collective-permute-start(bf16[320,128]{1,0:T(8,128)(2,1)S(1)} %get-tuple-element.7), channel_id=1, source_target_pairs={{1,2},{3,4},{5,6},{7,8},{9,10},{11,12},{13,14},{2,1},{4,3},{6,5},{... | collective-permute-start | bytes 245768 | tf_op jit(solution)/shard_map/ppermute | solution.py:280
  43.6 4.9 %collective-permute-start.1 = (bf16[320,128]{1,0:T(8,128)(2,1)S(1)}, bf16[320,128]{1,0:T(8,128)(2,1)S(1)}, u32[]{:S(2)}, u32[]{:S(2)}) collective-permute-start(bf16[320,128]{1,0:T(8,128)(2,1)S(1)} %get-tuple-element.8), channel_id=1, source_target_pairs={{0,1},{2,3},{4,5},{6,7},{8,9},{10,11},{12,13},{14,15},{1,0},{3,2},... | collective-permute-start | bytes 245768 | tf_op jit(solution)/shard_map/ppermute | solution.py:280
  48.5 0.0 copy-done.1
  48.5 1.0 %own.1.sums_ref = f32[4,256,256]{2,1,0:T(8,128)S(1)} custom-call(bf16[256,640]{1,0:T(8,128)(2,1)S(1)} %bitcast.7, f32[2,8,768]{2,1,0:T(8,128)S(1)} %copy-done.1), custom_call_target="tpu_custom_call" | custom-call | flops 1073741824 | bytes 1048576 | tf_op jit(solution)/shard_map/own/pallas_call | solution.py:248
  49.5 0.3 collective-permute-done.far_ref
  49.8 0.0 collective-permute-done.1.near_ref
  49.8 1.1 %finish.1 = bf16[32,64,128]{2,1,0:T(8,128)(2,1)S(1)} custom-call(f32[4,256,256]{2,1,0:T(8,128)S(1)} %own.1.sums_ref, bf16[320,128]{1,0:T(8,128)(2,1)S(1)} %collective-permute-done.far_ref, bf16[320,128]{1,0:T(8,128)(2,1)S(1)} %collective-permute-done.1.near_ref, f32[2,8,768]{2,1,0:T(8,128)S(1)} %copy-done.1), custom_call_target="tpu_custom_call" | custom-call | flops 1073741824 | bytes 1048576 | tf_op jit(solution)/shard_map/finish/pallas_call | solution.py:248
  50.9 36.6 %all_to_all.11 = bf16[32,64,128]{2,1,0:T(8,128)(2,1)S(1)} all-to-all(bf16[32,64,128]{2,1,0:T(8,128)(2,1)S(1)} %finish.1), channel_id=1, replica_groups=mesh['date'=32,'row'=16] {'date'}, dimensions={0} | all-to-all | bytes 1048576 | tf_op jit(solution)/shard_map/all_to_all | solution.py:276
  87.5 1.5 %spread.1 = f32[8,256,128]{2,1,0:T(8,128)} custom-call(bf16[2048,128]{1,0:T(8,128)(2,1)S(1)} %bitcast.5), custom_call_target="tpu_custom_call" | custom-call | bytes 1048576 | tf_op jit(solution)/shard_map/spread/pallas_call | solution.py:248
Async XLA Ops:
  0.0 0.9 %copy-start = (bf16[2,4,16,1024]{3,2,1,0:T(8,128)(2,1)S(1)}, bf16[2,4,16,1024]{3,2,1,0:T(8,128)(2,1)}, u32[]{:S(2)}) copy-start(bf16[2,4,16,1024]{3,2,1,0:T(8,128)(2,1)} %param.2) | copy-start | bytes 786436
  41.5 7.0 %copy-start.1 = (f32[2,8,768]{2,1,0:T(8,128)S(1)}, f32[2,8,768]{2,1,0:T(8,128)}, u32[]{:S(2)}) copy-start(f32[2,8,768]{2,1,0:T(8,128)} %constant.2.clone.masks_ref) | copy-start | bytes 147460
  41.6 8.2 %collective-permute-start = (bf16[320,128]{1,0:T(8,128)(2,1)S(1)}, bf16[320,128]{1,0:T(8,128)(2,1)S(1)}, u32[]{:S(2)}, u32[]{:S(2)}) collective-permute-start(bf16[320,128]{1,0:T(8,128)(2,1)S(1)} %get-tuple-element.7), channel_id=1, source_target_pairs={{1,2},{3,4},{5,6},{7,8},{9,10},{11,12},{13,14},{2,1},{4,3},{6,5},{... | collective-permute-start | bytes 245768 | tf_op jit(solution)/shard_map/ppermute | solution.py:280
  43.6 6.2 %collective-permute-start.1 = (bf16[320,128]{1,0:T(8,128)(2,1)S(1)}, bf16[320,128]{1,0:T(8,128)(2,1)S(1)}, u32[]{:S(2)}, u32[]{:S(2)}) collective-permute-start(bf16[320,128]{1,0:T(8,128)(2,1)S(1)} %get-tuple-element.8), channel_id=1, source_target_pairs={{0,1},{2,3},{4,5},{6,7},{8,9},{10,11},{12,13},{14,15},{1,0},{3,2},... | collective-permute-start | bytes 245768 | tf_op jit(solution)/shard_map/ppermute | solution.py:280

commit v5 on v4

--- a/solution.py
+++ b/solution.py
@@ -231,9 +231,10 @@
         moved = decode(moved)
         for y in range(2):
             results[k, pl.ds(y, dates, stride=2), :] = moved[:, cols * y:cols * (y + 1)]
-        if k % 2:
-            pair = pl.ds(k - 1, 2)
-            copies.append(pltpu.make_async_copy(results.at[pair], out_ref.at[pair], sems.at[k // 2]))
+        if k in (3, 6, 7):
+            start = {3: 0, 6: 4, 7: 7}[k]
+            ready = pl.ds(start, k + 1 - start)
+            copies.append(pltpu.make_async_copy(results.at[ready], out_ref.at[ready], sems.at[len(copies)]))
             copies[-1].start()
     for copy in copies:
         copy.wait()

time: 89.3 us -> 89.3 us (level)
  no operation moved by 1% of the time
where the time goes in v5:
time: 89.3 us; the launch traced here: 89.1 us
  blocking collectives  76.6 us (86%)
  starting transfers between devices  6.84 us (8%)
  Pallas kernels  4.3 us (5%)
  local copies, waits for them, and re-layouts  0.95 us (1%)
    all_to_all x2, blocking collectives, exchange(): lax.all_to_all(blocks, 'date', 0, 0, tiled=True)  76.6 us
    ppermute x2, starting transfers between devices, swapped(): return lax.ppermute(array, 'row', pairs + [(j, i) for i, j in pairs])  6.84 us
    pallas_call x5, Pallas kernels, run(): pl.pallas_call(kernel, out_shape=[jax.ShapeDtypeStruct(*shape) for shape...  4.3 us
  transfers between devices with their start and end apart: 2, of which 1 were waited for; matrix products, arithmetic and copies ran while one was open for 0% of the time, Pallas kernels for 1%

profile of v5, /device:TPU:36, one launch (start us, length us, event | category | flops | bytes accessed | tf_op | source)
XLA Modules:
  0.0 89.1 jit_solution(7547054375632217637)
XLA Ops:
  0.0 0.0 copy-start
  0.0 0.9 %copy-done = bf16[2,4,16,1024]{3,2,1,0:T(8,128)(2,1)S(1)} copy-done((bf16[2,4,16,1024]{3,2,1,0:T(8,128)(2,1)S(1)}, bf16[2,4,16,1024]{3,2,1,0:T(8,128)(2,1)}, u32[]{:S(2)}) %copy-start) | copy-done | bytes 262168
  1.0 0.5 pack.1
  1.4 40.0 %all_to_all.10 = bf16[32,8,640]{2,1,0:T(8,128)(2,1)S(1)} all-to-all(bf16[32,8,640]{2,1,0:T(8,128)(2,1)S(1)} %bitcast.8), channel_id=1, replica_groups=mesh['date'=32,'row'=16] {'date'}, dimensions={0} | all-to-all | bytes 655360 | tf_op jit(solution)/shard_map/all_to_all | solution.py:277
  41.5 0.0 copy-start.1
  41.5 0.2 message.1
  41.6 1.9 %collective-permute-start = (bf16[320,128]{1,0:T(8,128)(2,1)S(1)}, bf16[320,128]{1,0:T(8,128)(2,1)S(1)}, u32[]{:S(2)}, u32[]{:S(2)}) collective-permute-start(bf16[320,128]{1,0:T(8,128)(2,1)S(1)} %get-tuple-element.7), channel_id=1, source_target_pairs={{1,2},{3,4},{5,6},{7,8},{9,10},{11,12},{13,14},{2,1},{4,3},{6,5},{... | collective-permute-start | bytes 245768 | tf_op jit(solution)/shard_map/ppermute | solution.py:281
  43.6 4.9 %collective-permute-start.1 = (bf16[320,128]{1,0:T(8,128)(2,1)S(1)}, bf16[320,128]{1,0:T(8,128)(2,1)S(1)}, u32[]{:S(2)}, u32[]{:S(2)}) collective-permute-start(bf16[320,128]{1,0:T(8,128)(2,1)S(1)} %get-tuple-element.8), channel_id=1, source_target_pairs={{0,1},{2,3},{4,5},{6,7},{8,9},{10,11},{12,13},{14,15},{1,0},{3,2},... | collective-permute-start | bytes 245768 | tf_op jit(solution)/shard_map/ppermute | solution.py:281
  48.5 0.0 copy-done.1
  48.5 1.0 %own.1.sums_ref = f32[4,256,256]{2,1,0:T(8,128)S(1)} custom-call(bf16[256,640]{1,0:T(8,128)(2,1)S(1)} %bitcast.7, f32[2,8,768]{2,1,0:T(8,128)S(1)} %copy-done.1), custom_call_target="tpu_custom_call" | custom-call | flops 1073741824 | bytes 1048576 | tf_op jit(solution)/shard_map/own/pallas_call | solution.py:249
  49.5 0.3 collective-permute-done.far_ref
  49.8 0.0 collective-permute-done.1.near_ref
  49.8 1.1 %finish.1 = bf16[32,64,128]{2,1,0:T(8,128)(2,1)S(1)} custom-call(f32[4,256,256]{2,1,0:T(8,128)S(1)} %own.1.sums_ref, bf16[320,128]{1,0:T(8,128)(2,1)S(1)} %collective-permute-done.far_ref, bf16[320,128]{1,0:T(8,128)(2,1)S(1)} %collective-permute-done.1.near_ref, f32[2,8,768]{2,1,0:T(8,128)S(1)} %copy-done.1), custom_call_target="tpu_custom_call" | custom-call | flops 1073741824 | bytes 1048576 | tf_op jit(solution)/shard_map/finish/pallas_call | solution.py:249
  50.9 36.6 %all_to_all.11 = bf16[32,64,128]{2,1,0:T(8,128)(2,1)S(1)} all-to-all(bf16[32,64,128]{2,1,0:T(8,128)(2,1)S(1)} %finish.1), channel_id=1, replica_groups=mesh['date'=32,'row'=16] {'date'}, dimensions={0} | all-to-all | bytes 1048576 | tf_op jit(solution)/shard_map/all_to_all | solution.py:277
  87.5 1.6 %spread.1 = f32[8,256,128]{2,1,0:T(8,128)} custom-call(bf16[2048,128]{1,0:T(8,128)(2,1)S(1)} %bitcast.5), custom_call_target="tpu_custom_call" | custom-call | bytes 1048576 | tf_op jit(solution)/shard_map/spread/pallas_call | solution.py:249
Async XLA Ops:
  0.0 0.9 %copy-start = (bf16[2,4,16,1024]{3,2,1,0:T(8,128)(2,1)S(1)}, bf16[2,4,16,1024]{3,2,1,0:T(8,128)(2,1)}, u32[]{:S(2)}) copy-start(bf16[2,4,16,1024]{3,2,1,0:T(8,128)(2,1)} %param.2) | copy-start | bytes 786436
  41.5 7.0 %copy-start.1 = (f32[2,8,768]{2,1,0:T(8,128)S(1)}, f32[2,8,768]{2,1,0:T(8,128)}, u32[]{:S(2)}) copy-start(f32[2,8,768]{2,1,0:T(8,128)} %constant.2.clone.masks_ref) | copy-start | bytes 147460
  41.6 8.2 %collective-permute-start = (bf16[320,128]{1,0:T(8,128)(2,1)S(1)}, bf16[320,128]{1,0:T(8,128)(2,1)S(1)}, u32[]{:S(2)}, u32[]{:S(2)}) collective-permute-start(bf16[320,128]{1,0:T(8,128)(2,1)S(1)} %get-tuple-element.7), channel_id=1, source_target_pairs={{1,2},{3,4},{5,6},{7,8},{9,10},{11,12},{13,14},{2,1},{4,3},{6,5},{... | collective-permute-start | bytes 245768 | tf_op jit(solution)/shard_map/ppermute | solution.py:281
  43.6 6.2 %collective-permute-start.1 = (bf16[320,128]{1,0:T(8,128)(2,1)S(1)}, bf16[320,128]{1,0:T(8,128)(2,1)S(1)}, u32[]{:S(2)}, u32[]{:S(2)}) collective-permute-start(bf16[320,128]{1,0:T(8,128)(2,1)S(1)} %get-tuple-element.8), channel_id=1, source_target_pairs={{0,1},{2,3},{4,5},{6,7},{8,9},{10,11},{12,13},{14,15},{1,0},{3,2},... | collective-permute-start | bytes 245768 | tf_op jit(solution)/shard_map/ppermute | solution.py:281
